TPU v7x, 512 devices: a whole 4x4x16 slice. The times are simulated.
512 devices in a mesh: wide: 16 (over x, z_hi), long: 32 (over z_lo, y, core).
Axes of the slice: x: 4, y: 4, z: 16 (z_hi: 4, z_lo: 4; z = z_hi * 4 + z_lo), core: 2. Of those that a mesh axis runs over, the one named last changes fastest.
Arguments:
- velocity: bfloat16 [3, 128, 1024, 512], P(None, 'wide', 'long'), may hold values from -6 to 6
- vorticity: bfloat16 [3, 128, 1024, 512], P(None, 'wide', 'long'), may hold values from -6 to 6
- m_of_slot: int32 [512], replicated, may hold values from 0 to 511, as said below
- legendre: bfloat16 [512, 512, 512], P('long', 'wide'), as said below
- known_term: bfloat16 [512, 2, 3, 512, 128], P('long', None, None, 'wide'), may hold values from -6 to 6
- inverse: bfloat16 [512, 128, 128], P('wide'), may hold values from -0.5 to 0.5
Outputs:
- section_state: bfloat16 [512, 2, 3, 512, 128], P('long', None, None, 'wide')
Inputs may be any that keep to these rules, and one draw needn't show every extreme that they name: m_of_slot is a permutation of 0 to 511; the m of slot s differs from s by less than 32. legendre[s, l, t] is zero wherever the degree l is below m_of_slot[s].
All inputs are finite; a program needn't handle non-finite values.
Results may differ from a plain program's by a relative error of at most 0.0059.
Values may be sent and summed in bfloat16 or wider, within the bound.
No kernel may reach another device: no remote copies, remote signals or barrier semaphores. Data moves between devices by JAX's collectives and lax.ppermute only.
A program may use at most 192 MiB of HBM per device.

v0:
```python
import math
import jax
import jax.numpy as jnp
from jax import lax
from jax.sharding import PartitionSpec as P

section_step = 0.75


def lamb_product(velocity, vorticity):
    vel = velocity.astype(jnp.float32)
    vort = vorticity.astype(jnp.float32)
    first = vel[1] * vort[2] - vel[2] * vort[1]
    second = vel[2] * vort[0] - vel[0] * vort[2]
    third = vel[0] * vort[1] - vel[1] * vort[0]
    return jnp.stack([first, second, third], axis=0).astype(jnp.bfloat16)


def phase_table(m_of_slot, points):
    column = jnp.arange(points, dtype=jnp.int32)
    paired_modes = jnp.repeat(m_of_slot, 2)
    parity = jnp.arange(paired_modes.shape[0], dtype=jnp.int32) % 2
    product = column[:, None] * paired_modes[None, :] % points
    phase_angle = 2.0 * math.pi / points * product.astype(jnp.float32)
    norm_factor = math.sqrt(2.0 / points)
    values = jnp.where(
        parity[None, :] == 0,
        norm_factor * jnp.cos(phase_angle),
        -norm_factor * jnp.sin(phase_angle),
    )
    return values.astype(jnp.bfloat16)


def body(velocity, vorticity, m_of_slot, legendre, known_term, inverse):
    lamb_vector = lamb_product(velocity, vorticity)
    full_phi = lax.all_to_all(lamb_vector, "long", split_axis=3, concat_axis=2, tiled=True)
    table_local = phase_table(m_of_slot, full_phi.shape[2])
    fourier = jnp.einsum(
        "frjt,jc->frct", full_phi, table_local, preferred_element_type=jnp.float32
    ).astype(jnp.bfloat16)
    slot_major = lax.all_to_all(fourier, "long", split_axis=2, concat_axis=3, tiled=True)
    slot_count = legendre.shape[0]
    nodes = slot_major.shape[3]
    piece = lax.all_gather(slot_major, "wide", axis=1, tiled=True)
    piece_block = piece.reshape(3, piece.shape[1], slot_count, 2, nodes)
    summed = jnp.einsum(
        "frsct,slt->scflr", piece_block, legendre, preferred_element_type=jnp.float32
    )
    coeffs = summed.astype(jnp.bfloat16)
    coeffs = lax.optimization_barrier(coeffs)
    right_side = (
        known_term.astype(jnp.float32) + section_step * coeffs.astype(jnp.float32)
    ).astype(jnp.bfloat16)
    solved = jnp.einsum("scflr,lqr->scflq", right_side, inverse, preferred_element_type=jnp.float32)
    return solved.astype(jnp.bfloat16)


def solution(mesh):
    return jax.shard_map(
        body,
        mesh=mesh,
        in_specs=(
            P(None, "wide", "long", None),
            P(None, "wide", "long", None),
            P(),
            P("long", "wide", None),
            P("long", None, None, "wide", None),
            P("wide", None, None),
        ),
        out_specs=P("long", None, None, "wide", None),
        check_vma=False,
    )
```

profile of v0, /device:TPU:1, one launch (start us, length us, event | category | flops | bytes accessed | tf_op | source)
XLA Modules:
  0.0 1266.5 jit_solution(17308692861983787634)
XLA Ops:
  6.5 0.0 copy-start
  6.5 1.4 convert_element_type.43
  8.0 1.3 convert_element_type.44
  9.3 0.5 subtract_convert_fusion.2
  9.8 0.1 pad_maximum_fusion
  9.9 0.0 copy-start.3
  9.9 3.6 copy.24
  13.5 5.8 reshape.19
  19.3 10.4 all-to-all-start
  29.7 0.2 all-gather.2.cloned.1.call-start
  29.9 0.0 copy-done.3
  30.0 0.1 broadcast_in_dim.14
  30.1 0.2 mul.64
  30.3 21.1 %all-to-all-done = bf16[32,2,6144]{2,1,0:T(2,128)(2,1)S(1)} async-done(((bf16[32,2,6144]{2,1,0:T(2,128)(2,1)}), bf16[32,2,6144]{2,1,0:T(2,128)(2,1)S(1)}, u32[]{:S(2)}, u32[]{:S(2)}) %all-to-all-start) | async-done | bytes 786464 | tf_op jit(solution)/shard_map/all_to_all | solution.py:36
  51.4 2.7 reshape.20
  54.0 5.6 copy.26
  59.6 4.8 all_to_all.29
  64.5 17.9 %fusion.20 = bf16[3,8,1024,16]{2,3,1,0:T(8,128)(2,1)S(1)} fusion(bf16[3,8,1024,16]{2,3,1,0:T(8,128)(2,1)S(1)} %all_to_all.29, s32[1024]{0:T(1024)S(1)} %mul.64, pred[1024]{0:T(1024)(128)(4,1)S(1)} %fusion.28), kind=kOutput, calls=%fused_computation.24 | convolution fusion | flops 824573952 | bytes 1577984 | tf_op jit(solution)/shard_map/frjt,jc->frct/dot_general | solution.py:38
  82.3 6.1 copy.27
  88.4 8.9 reshape.21
  97.3 25.9 %all_to_all.36 = bf16[32,2,6144]{2,1,0:T(2,128)(2,1)S(1)} all-to-all(bf16[32,2,6144]{2,1,0:T(2,128)(2,1)S(1)} %reshape.21), channel_id=1, replica_groups=mesh['wide'=16,'long'=32] {'long'}, dimensions={0} | all-to-all | bytes 1572864 | tf_op jit(solution)/shard_map/all_to_all | solution.py:41
  123.2 5.6 reshape.22
  128.8 7.7 copy.28
  136.5 0.0 all-gather.2.cloned.1.call-update
  136.5 0.0 copy-start.2
  136.5 1068.2 %all-gather.2.cloned.1.call-done = bf16[3,128,32,512]{2,3,1,0:T(8,128)(2,1)} async-done(((bf16[3,8,32,512]{2,3,1,0:T(8,128)(2,1)}), bf16[3,128,32,512]{2,3,1,0:T(8,128)(2,1)}) %all-gather.2.cloned.1.call-update) | async-done | bytes 12582928 | tf_op jit(solution)/shard_map/all_gather | solution.py:44
  1204.7 45.8 %copy.37 = bf16[3,128,32,512]{3,1,0,2:T(8,128)(2,1)} copy(bf16[3,128,32,512]{2,3,1,0:T(8,128)(2,1)} %all-gather.2.cloned.1.call-done) | data formatting | bytes 25165824 | tf_op jit(solution)/shard_map/reshape | solution.py:45
  1250.6 6.8 fusion.24
  1257.4 0.0 copy-done.1
  1257.4 0.3 add_convert_fusion
  1257.7 0.8 fusion.23
  1258.5 1.2 copy.32
  (4 shorter events, 0.0 us)
Async XLA Ops:
  6.5 1251.2 %copy-start = (bf16[32,128,128]{2,1,0:T(8,128)(2,1)S(1)}, bf16[32,128,128]{2,1,0:T(8,128)(2,1)}, u32[]{:S(2)}) copy-start(bf16[32,128,128]{2,1,0:T(8,128)(2,1)} %param.11) | copy-start | bytes 3145732
  9.9 20.1 %copy-start.3 = (s32[512]{0:T(512)S(1)}, s32[512]{0:T(512)}, u32[]{:S(2)}) copy-start(s32[512]{0:T(512)} %param.8) | copy-start | bytes 6148
  19.3 32.1 %all-to-all-start = ((bf16[32,2,6144]{2,1,0:T(2,128)(2,1)}), bf16[32,2,6144]{2,1,0:T(2,128)(2,1)S(1)}, u32[]{:S(2)}, u32[]{:S(2)}) async-start(bf16[32,2,6144]{2,1,0:T(2,128)(2,1)} %reshape.19), calls=%async_computation | async-start | bytes 1572864 | tf_op jit(solution)/shard_map/all_to_all | solution.py:36
  29.7 1175.0 %all-gather.2.cloned.1.call-start = ((), (), s32[]{:S(2)}) async-start(), calls=%async_computation.2 | async-start | bytes 53477376 | tf_op jit(solution)/shard_map/all_gather | solution.py:44
  136.5 1114.0 %copy-start.2 = (bf16[16,32,512]{2,1,0:T(8,128)(2,1)S(1)}, bf16[16,32,512]{2,1,0:T(8,128)(2,1)}, u32[]{:S(2)}) copy-start(bf16[16,32,512]{2,1,0:T(8,128)(2,1)} %param.9) | copy-start | bytes 1572868
  1250.5 6.9 copy-start.1
Sparse Core Ops, SparseCore 0:
  136.6 1068.0 all-gather.1
where the time goes:
time: 1270 us
  waiting for transfers between devices  1090 us (86%)
  local copies, waits for them, and re-layouts  98.1 us (8%)
  blocking collectives  25.9 us (2%)
  matrix products  25.5 us (2%)
  between operations  13.5 us (1%)
    all_gather x1, waiting for transfers between devices, body(): piece = lax.all_gather(slot_major, 'wide', axis=1, tiled=True)  1070 us
    reshape x1, local copies, waits for them, and re-layouts, body(): piece_block = piece.reshape(3, piece.shape[1], slot_count, 2, nodes)  45.8 us
    all_to_all x1, blocking collectives, body(): lax.all_to_all(fourier, 'long', split_axis=2, concat_axis=3, tiled=True)  25.9 us
  transfers between devices with their start and end apart: 2, of which 2 were waited for; matrix products, arithmetic and copies ran while one was open for 0% of the time, Pallas kernels for 0%

commit v1 on v0

--- a/solution.py
+++ b/solution.py
@@ -41,7 +41,15 @@
     slot_major = lax.all_to_all(fourier, "long", split_axis=2, concat_axis=3, tiled=True)
     slot_count = legendre.shape[0]
     nodes = slot_major.shape[3]
-    piece = lax.all_gather(slot_major, "wide", axis=1, tiled=True)
+    piece = jnp.concatenate(
+        lax.all_to_all(
+            jnp.stack([slot_major for _ in range(lax.psum(1, axis_name="wide"))]),
+            axis_name="wide",
+            split_axis=0,
+            concat_axis=0,
+        ),
+        axis=1,
+    )
     piece_block = piece.reshape(3, piece.shape[1], slot_count, 2, nodes)
     summed = jnp.einsum(
         "frsct,slt->scflr", piece_block, legendre, preferred_element_type=jnp.float32

time: 1270 us -> 726 us (0.57)
  waiting for transfers between devices: 1090 us -> 21.3 us
  blocking collectives: 25.9 us -> 589 us
  local copies, waits for them, and re-layouts: 98.1 us -> 67 us
  between operations: 13.5 us -> 0.15 us
    all_gather x1 -> x0, waiting for transfers between devices: 1070 us -> none  [body(): piece = lax.all_gather(slot_major, 'wide', axis=1, tiled=True)]
    all_to_all x0 -> x1, blocking collectives: none -> 563 us  [body(): lax.all_to_all(jnp.stack([slot_major for _ in range(lax.psum(1, axis_name...]
    reshape x1 -> x0, local copies, waits for them, and re-layouts: 45.8 us -> none  [body(): piece_block = piece.reshape(3, piece.shape[1], slot_count, 2, nodes)]
  transfers between devices with their start and end apart: 2 -> 1, of which waited for: 2 -> 1; matrix products, arithmetic and copies ran while one was open for 0% -> 0% of each run, Pallas kernels for 0% -> 0%
where the time goes in v1:
time: 726 us; the launch traced here: 717 us
  blocking collectives  589 us (81%)
  local copies, waits for them, and re-layouts  67 us (9%)
  matrix products  25.5 us (4%)
  waiting for transfers between devices  21.3 us (3%)
  starting transfers between devices  10.5 us (1%)
    all_to_all x1, blocking collectives, body(): lax.all_to_all(jnp.stack([slot_major for _ in range(lax.psum(1, axis_name...  563 us
    all_to_all x1, blocking collectives, body(): lax.all_to_all(fourier, 'long', split_axis=2, concat_axis=3, tiled=True)  25.9 us
    unnamed x12, local copies, waits for them, and re-layouts  23 us
    all_to_all x1, waiting for transfers between devices, body(): lax.all_to_all(lamb_vector, 'long', split_axis=3, concat_axis=2, tiled=True)  21.3 us
    dot_general x1, matrix products, body(): jnp.einsum('frjt,jc->frct', full_phi, table_local, preferred_element_type...  17.9 us
  transfers between devices with their start and end apart: 1, of which 1 were waited for; matrix products, arithmetic and copies ran while one was open for 0% of the time, Pallas kernels for 0%

profile of v1, /device:TPU:1, one launch (start us, length us, event | category | flops | bytes accessed | tf_op | source)
XLA Modules:
  0.0 716.7 jit_solution(11081832800527442826)
XLA Ops:
  0.0 0.0 copy-start
  0.0 1.4 convert_element_type.43
  1.4 1.3 convert_element_type.44
  2.8 0.5 subtract_convert_fusion.2
  3.3 0.1 pad_maximum_fusion
  3.4 0.0 copy-start.2
  3.4 3.6 copy.17
  6.9 5.8 reshape.22
  12.8 10.5 %all-to-all-start = ((bf16[32,2,6144]{2,1,0:T(2,128)(2,1)}), bf16[32,2,6144]{2,1,0:T(2,128)(2,1)S(1)}, u32[]{:S(2)}, u32[]{:S(2)}) async-start(bf16[32,2,6144]{2,1,0:T(2,128)(2,1)} %reshape.22), calls=%async_computation | async-start | bytes 1572864 | tf_op jit(solution)/shard_map/all_to_all | solution.py:36
  23.2 0.0 copy-done.2
  23.2 0.1 broadcast_in_dim.14
  23.3 0.2 mul.64
  23.5 21.3 %all-to-all-done = bf16[32,2,6144]{2,1,0:T(2,128)(2,1)S(1)} async-done(((bf16[32,2,6144]{2,1,0:T(2,128)(2,1)}), bf16[32,2,6144]{2,1,0:T(2,128)(2,1)S(1)}, u32[]{:S(2)}, u32[]{:S(2)}) %all-to-all-start) | async-done | bytes 786464 | tf_op jit(solution)/shard_map/all_to_all | solution.py:36
  44.9 2.7 reshape.23
  47.5 5.6 copy.19
  53.1 4.8 all_to_all.30
  58.0 17.9 %fusion.28 = bf16[3,8,1024,16]{2,3,1,0:T(8,128)(2,1)S(1)} fusion(bf16[3,8,1024,16]{2,3,1,0:T(8,128)(2,1)S(1)} %all_to_all.30, s32[1024]{0:T(1024)S(1)} %mul.64, pred[1024]{0:T(1024)(128)(4,1)S(1)} %fusion.35), kind=kOutput, calls=%fused_computation.27 | convolution fusion | flops 824573952 | bytes 1577984 | tf_op jit(solution)/shard_map/frjt,jc->frct/dot_general | solution.py:38
  75.8 6.1 copy.20
  81.9 8.9 %reshape.24 = bf16[32,2,6144]{2,1,0:T(2,128)(2,1)S(1)} reshape(bf16[1024,3,8,16]{3,2,1,0:T(8,128)(2,1)} %bitcast.44) | data formatting | bytes 1572864
  90.8 25.9 %all_to_all.38 = bf16[32,2,6144]{2,1,0:T(2,128)(2,1)S(1)} all-to-all(bf16[32,2,6144]{2,1,0:T(2,128)(2,1)S(1)} %reshape.24), channel_id=1, replica_groups=mesh['wide'=16,'long'=32] {'long'}, dimensions={0} | all-to-all | bytes 1572864 | tf_op jit(solution)/shard_map/all_to_all | solution.py:41
  116.7 5.6 reshape.25
  122.3 7.7 %copy.21 = bf16[3,8,32,32,16]{3,4,2,1,0:T(8,128)(2,1)} copy(bf16[3,8,32,32,16]{4,1,0,3,2:T(8,128)(2,1)} %bitcast.45) | data formatting | bytes 1572864 | tf_op jit(solution)/shard_map/all_to_all | solution.py:41
  130.0 3.4 copy.22
  133.4 6.0 stack.9
  139.4 562.8 %all_to_all.39 = bf16[16,3,8,32,512]{4,2,3,1,0:T(8,128)(2,1)S(1)} all-to-all(bf16[16,3,8,32,512]{4,2,3,1,0:T(8,128)(2,1)} %stack.9), channel_id=1, replica_groups=mesh['wide'=16,'long'=32] {'wide'}, dimensions={0} | all-to-all | bytes 25165824 | tf_op jit(solution)/shard_map/all_to_all | solution.py:45
  702.2 5.3 copy.23
  707.5 0.0 copy-done.3
  707.6 6.8 fusion.25
  714.4 0.3 add_convert_fusion
  714.7 0.0 copy-done
  714.7 0.8 fusion.31
  715.5 1.2 copy.26
  (4 shorter events, 0.0 us)
Async XLA Ops:
  0.0 714.7 %copy-start = (bf16[32,128,128]{2,1,0:T(8,128)(2,1)S(1)}, bf16[32,128,128]{2,1,0:T(8,128)(2,1)}, u32[]{:S(2)}) copy-start(bf16[32,128,128]{2,1,0:T(8,128)(2,1)} %param.11) | copy-start | bytes 3145732
  3.4 19.8 %copy-start.2 = (s32[512]{0:T(512)S(1)}, s32[512]{0:T(512)}, u32[]{:S(2)}) copy-start(s32[512]{0:T(512)} %param.8) | copy-start | bytes 6148
  12.8 32.1 %all-to-all-start = ((bf16[32,2,6144]{2,1,0:T(2,128)(2,1)}), bf16[32,2,6144]{2,1,0:T(2,128)(2,1)S(1)}, u32[]{:S(2)}, u32[]{:S(2)}) async-start(bf16[32,2,6144]{2,1,0:T(2,128)(2,1)} %reshape.22), calls=%async_computation | async-start | bytes 1572864 | tf_op jit(solution)/shard_map/all_to_all | solution.py:36
  702.2 5.3 copy-start.3
  707.5 6.9 copy-start.1
